TPU v7x, 32 devices: a whole 2x2x4 slice. The times are simulated.
32 devices in a mesh: dp: 2 (over core), row: 4 (over z), col: 4 (over y, x).
Axes of the slice: x: 2, y: 2, z: 4, core: 2. Of those that a mesh axis runs over, the one named last changes fastest.
Arguments:
- tokens: float32 [16384, 2048], P(('dp', 'col'), 'row'), may hold values from -6 to 6
- segments: int32 [8, 2048], P(('dp', 'col')), may hold values from 0 to 15, never falling along the last dimension, each value on 1 to 1024 neighbouring positions
- cotangent: float32 [16384, 2048], P(('dp', 'col'), 'row'), may hold values from -6 to 6
- w_query: bfloat16 [2048, 2048], P('col', 'row'), may hold values from -0.125 to 0.125
- w_key: bfloat16 [2048, 512], P('col', 'row'), may hold values from -0.125 to 0.125
- w_value: bfloat16 [2048, 512], P('col', 'row'), may hold values from -0.125 to 0.125
- w_out: bfloat16 [2048, 2048], P('row', 'col'), may hold values from -1 to 1
- w_gate: bfloat16 [2048, 8192], P('col', 'row'), may hold values from -0.125 to 0.125
- w_up: bfloat16 [2048, 8192], P('col', 'row'), may hold values from -0.125 to 0.125
- w_down: bfloat16 [8192, 2048], P('row', 'col'), may hold values from -0.0625 to 0.0625
- gain_attn: float32 [2048], P('row'), may hold values from 0.5 to 1.5
- gain_mlp: float32 [2048], P('row'), may hold values from 0.5 to 1.5
Outputs:
- hidden_out: float32 [16384, 2048], P(('dp', 'col'), 'row')
- grad_tokens: float32 [16384, 2048], P(('dp', 'col'), 'row')
- grad_w_query: float32 [2048, 2048], P('col', 'row')
- grad_w_key: float32 [2048, 512], P('col', 'row')
- grad_w_value: float32 [2048, 512], P('col', 'row')
- grad_w_out: float32 [2048, 2048], P('row', 'col')
- grad_w_gate: float32 [2048, 8192], P('col', 'row')
- grad_w_up: float32 [2048, 8192], P('col', 'row')
- grad_w_down: float32 [8192, 2048], P('row', 'col')
- grad_gain_attn: float32 [2048], P('row')
- grad_gain_mlp: float32 [2048], P('row')
Inputs may be any that keep to these rules, and one draw needn't show every extreme that they name: `segments`: in each row the document numbers never fall; each document has 1 to 1024 tokens, one exactly 1024.
All inputs are finite; a program needn't handle non-finite values.
Results may differ from a plain program's by a relative error of at most 0.013.
Values may be sent and summed in bfloat16 or wider, within the bound.
A program may use at most 384 MiB of HBM per device.

v0:
```python
import math

import jax
import jax.numpy as jnp
from jax import lax
from jax.sharding import PartitionSpec as P

D = 2048
HEADS = 32
KV = 8
HD = 64
QBLOCK = 512


NORM_EPS = 1e-05
ROPE_BASE = 500000.0
MASK_FILL = -1e30


def feature_sum(values):
    return lax.psum(values, "row")


def gather_features(values):
    return lax.all_gather(values, "row", axis=1, tiled=True)


def reduce_features(values):
    return lax.psum_scatter(values, "row", scatter_dimension=1, tiled=True)


def positions(segment_row):
    token_ids = jnp.arange(segment_row.shape[0], dtype=jnp.int32)
    starts = jnp.concatenate([jnp.ones((1,), dtype=jnp.bool_), segment_row[1:] != segment_row[:-1]])
    doc_start = lax.cummax(jnp.where(starts, token_ids, 0), axis=0)
    return token_ids - doc_start


def rope_tables(places):
    inverse = ROPE_BASE ** (-jnp.arange(HD // 2, dtype=jnp.float32) * 2.0 / HD)
    angles = places.astype(jnp.float32)[:, None] * inverse[None, :]
    return (jnp.cos(angles)[:, None, :], jnp.sin(angles)[:, None, :])


def rotate(values, cosine, sine_part):
    half_width = values.shape[-1] // 2
    first_half = values[..., :half_width]
    second_half = values[..., half_width:]
    return jnp.concatenate(
        [
            first_half * cosine - second_half * sine_part,
            second_half * cosine + first_half * sine_part,
        ],
        axis=-1,
    )


def norm_forward(tokens_in, gain_row):
    totals = feature_sum(jnp.sum(tokens_in * tokens_in, axis=1))
    scale_rows = lax.rsqrt(totals / D + NORM_EPS)[:, None]
    return (scale_rows, (tokens_in * scale_rows * gain_row).astype(jnp.bfloat16))


def norm_backward(tokens_in, scale_rows, gain_row, grad_normed):
    inner_sum = feature_sum(jnp.sum(grad_normed * gain_row * tokens_in, axis=1))[:, None]
    grad_in = scale_rows * gain_row * grad_normed - tokens_in * scale_rows**3 * inner_sum / D
    grad_gain = jnp.sum(grad_normed * tokens_in * scale_rows, axis=0)
    return (grad_in, grad_gain)


def block_scores(block_query, keys_rot, segment_row, block_start):
    length = segment_row.shape[0]
    token_ids = jnp.arange(length, dtype=jnp.int32)
    rows_at = block_start + jnp.arange(QBLOCK, dtype=jnp.int32)
    row_segments = lax.dynamic_slice_in_dim(segment_row, block_start, QBLOCK, 0)
    allowed = (rows_at[:, None] >= token_ids[None, :]) & (
        row_segments[:, None] == segment_row[None, :]
    )
    scores = jnp.einsum("qkgd,tkd->kgqt", block_query, keys_rot, preferred_element_type=jnp.float32)
    scores = scores * (1.0 / math.sqrt(HD))
    return jnp.where(allowed[None, None], scores, MASK_FILL)


def attend_forward(inputs):
    queries, keys_rot, values_low, segment_row = inputs
    blocks = queries.shape[0] // QBLOCK

    def one_block(block_number):
        block_start = block_number * QBLOCK
        block_query = lax.dynamic_slice_in_dim(queries, block_start, QBLOCK, 0)
        scores = block_scores(block_query, keys_rot, segment_row, block_start)
        row_max = jnp.max(scores, axis=-1, keepdims=True)
        exp_scores = jnp.exp(scores - row_max)
        row_total = jnp.sum(exp_scores, axis=-1, keepdims=True)
        probs_low = (exp_scores / row_total).astype(jnp.bfloat16)
        mixed_rows = jnp.einsum(
            "kgqt,tkd->qkgd", probs_low, values_low, preferred_element_type=jnp.float32
        )
        return (mixed_rows.astype(jnp.bfloat16), (row_max + jnp.log(row_total))[..., 0])

    return lax.map(one_block, jnp.arange(blocks, dtype=jnp.int32))


def attend_backward(inputs):
    queries, keys_rot, values_low, segment_row, log_sums, grad_mixed = inputs
    blocks = queries.shape[0] // QBLOCK
    score_scale = 1.0 / math.sqrt(HD)

    def one_block(running, block_inputs):
        grad_keys, grad_values = running
        block_number, block_lse, block_grad = block_inputs
        block_start = block_number * QBLOCK
        block_query = lax.dynamic_slice_in_dim(queries, block_start, QBLOCK, 0)
        scores = block_scores(block_query, keys_rot, segment_row, block_start)
        probs_full = jnp.exp(scores - block_lse[..., None])
        probs_low = probs_full.astype(jnp.bfloat16)
        grad_probs = jnp.einsum(
            "qkgd,tkd->kgqt", block_grad, values_low, preferred_element_type=jnp.float32
        )
        row_delta = jnp.sum(grad_probs * probs_full, axis=-1, keepdims=True)
        grad_scores = (probs_full * (grad_probs - row_delta)).astype(jnp.bfloat16)
        grad_query = (
            jnp.einsum("kgqt,tkd->qkgd", grad_scores, keys_rot, preferred_element_type=jnp.float32)
            * score_scale
        )
        grad_keys = (
            grad_keys
            + jnp.einsum(
                "kgqt,qkgd->tkd", grad_scores, block_query, preferred_element_type=jnp.float32
            )
            * score_scale
        )
        grad_values = grad_values + jnp.einsum(
            "kgqt,qkgd->tkd", probs_low, block_grad, preferred_element_type=jnp.float32
        )
        return ((grad_keys, grad_values), grad_query)

    empty = jnp.zeros(keys_rot.shape, jnp.float32)
    (grad_keys, grad_values), grad_queries = lax.scan(
        one_block, (empty, empty), (jnp.arange(blocks, dtype=jnp.int32), log_sums, grad_mixed)
    )
    return (grad_queries, grad_keys, grad_values)


def per_device(
    tokens,
    segments,
    cotangent,
    w_query,
    w_key,
    w_value,
    w_out,
    w_gate,
    w_up,
    w_down,
    gain_attn,
    gain_mlp,
):
    query_full, key_full, value_full, out_full, gate_full, up_full, down_full = (
        lax.all_gather(w_query, "col", axis=0, tiled=True),
        lax.all_gather(w_key, "col", axis=0, tiled=True),
        lax.all_gather(w_value, "col", axis=0, tiled=True),
        lax.all_gather(w_out, "col", axis=1, tiled=True),
        lax.all_gather(w_gate, "col", axis=0, tiled=True),
        lax.all_gather(w_up, "col", axis=0, tiled=True),
        lax.all_gather(w_down, "col", axis=1, tiled=True),
    )
    seq_count, length = segments.shape
    row_count = tokens.shape[0]
    blocks = length // QBLOCK
    heads_here = query_full.shape[1] // HD
    kv_here = key_full.shape[1] // HD
    group_size = HEADS // KV
    col_count = lax.axis_size("col")
    places = jax.vmap(positions)(segments).reshape(row_count)
    cosine, sine_part = rope_tables(places)
    scale_one, normed_local = norm_forward(tokens, gain_attn)
    normed_one = gather_features(normed_local)
    query_raw = jnp.dot(normed_one, query_full, preferred_element_type=jnp.float32).reshape(
        row_count, heads_here, HD
    )
    key_raw = jnp.dot(normed_one, key_full, preferred_element_type=jnp.float32).reshape(
        row_count, kv_here, HD
    )
    value_low = jnp.dot(normed_one, value_full, preferred_element_type=jnp.float32).astype(
        jnp.bfloat16
    )
    value_low = value_low.reshape(seq_count, length, kv_here, HD)
    query_rot = rotate(query_raw, cosine, sine_part).astype(jnp.bfloat16)
    query_rot = query_rot.reshape(seq_count, length, kv_here, group_size, HD)
    key_rot = (
        rotate(key_raw, cosine, sine_part)
        .astype(jnp.bfloat16)
        .reshape(seq_count, length, kv_here, HD)
    )
    mixed_blocks, log_sums = lax.map(attend_forward, (query_rot, key_rot, value_low, segments))
    mixed_low = mixed_blocks.reshape(row_count, heads_here * HD)
    attn_part = jnp.dot(mixed_low, out_full, preferred_element_type=jnp.float32)
    after_attn = tokens + reduce_features(attn_part)
    scale_two, normed_local_two = norm_forward(after_attn, gain_mlp)
    normed_two = gather_features(normed_local_two)
    gate_act = jnp.dot(normed_two, gate_full, preferred_element_type=jnp.float32)
    up_proj = jnp.dot(normed_two, up_full, preferred_element_type=jnp.float32)
    sigmoid_gate = jax.nn.sigmoid(gate_act)
    hidden = (gate_act * sigmoid_gate * up_proj).astype(jnp.bfloat16)
    result = after_attn + reduce_features(
        jnp.dot(hidden, down_full, preferred_element_type=jnp.float32)
    )
    grad_branch = gather_features(cotangent.astype(jnp.bfloat16))
    grad_down_w = jnp.einsum("tf,td->fd", hidden, grad_branch, preferred_element_type=jnp.float32)
    grad_hidden = jnp.einsum(
        "td,fd->tf", grad_branch, down_full, preferred_element_type=jnp.float32
    )
    grad_gate = (
        grad_hidden * up_proj * sigmoid_gate * (1.0 + gate_act * (1.0 - sigmoid_gate))
    ).astype(jnp.bfloat16)
    grad_up = (grad_hidden * gate_act * sigmoid_gate).astype(jnp.bfloat16)
    grad_gate_w = jnp.einsum("td,tf->df", normed_two, grad_gate, preferred_element_type=jnp.float32)
    grad_up_w = jnp.einsum("td,tf->df", normed_two, grad_up, preferred_element_type=jnp.float32)
    grad_normed_part = jnp.einsum(
        "tf,df->td", grad_gate, gate_full, preferred_element_type=jnp.float32
    )
    grad_normed_part = grad_normed_part + jnp.einsum(
        "tf,df->td", grad_up, up_full, preferred_element_type=jnp.float32
    )
    grad_normed_two = reduce_features(grad_normed_part)
    grad_after, grad_gain_two = norm_backward(after_attn, scale_two, gain_mlp, grad_normed_two)
    grad_after = cotangent + grad_after
    tile_mlp = jnp.broadcast_to(grad_gain_two[None, :], (col_count, grad_gain_two.shape[0]))
    grad_attn_branch = gather_features(grad_after.astype(jnp.bfloat16))
    grad_out_w = jnp.einsum(
        "th,td->hd", mixed_low, grad_attn_branch, preferred_element_type=jnp.float32
    )
    grad_mixed = jnp.einsum(
        "td,hd->th", grad_attn_branch, out_full, preferred_element_type=jnp.float32
    )
    grad_mixed = grad_mixed.astype(jnp.bfloat16).reshape(
        seq_count, blocks, QBLOCK, kv_here, group_size, HD
    )
    grad_query_blocks, grad_keys, grad_values = lax.map(
        attend_backward, (query_rot, key_rot, value_low, segments, log_sums, grad_mixed)
    )
    grad_query = rotate(grad_query_blocks.reshape(row_count, heads_here, HD), cosine, -sine_part)
    grad_query = grad_query.astype(jnp.bfloat16).reshape(row_count, heads_here * HD)
    grad_key = rotate(grad_keys.reshape(row_count, kv_here, HD), cosine, -sine_part)
    grad_key = grad_key.astype(jnp.bfloat16).reshape(row_count, kv_here * HD)
    grad_value = grad_values.reshape(row_count, kv_here * HD).astype(jnp.bfloat16)
    grad_query_w = jnp.einsum(
        "td,th->dh", normed_one, grad_query, preferred_element_type=jnp.float32
    )
    grad_key_w = jnp.einsum("td,th->dh", normed_one, grad_key, preferred_element_type=jnp.float32)
    grad_value_w = jnp.einsum(
        "td,th->dh", normed_one, grad_value, preferred_element_type=jnp.float32
    )
    grad_first = jnp.einsum("th,dh->td", grad_query, query_full, preferred_element_type=jnp.float32)
    grad_first = grad_first + jnp.einsum(
        "th,dh->td", grad_key, key_full, preferred_element_type=jnp.float32
    )
    grad_first = grad_first + jnp.einsum(
        "th,dh->td", grad_value, value_full, preferred_element_type=jnp.float32
    )
    grad_normed_one = reduce_features(grad_first)
    grad_before, grad_gain_one = norm_backward(tokens, scale_one, gain_attn, grad_normed_one)
    grad_input = grad_after + grad_before
    tile_attn = jnp.broadcast_to(grad_gain_one[None, :], (col_count, grad_gain_one.shape[0]))
    col_summed = (
        lax.psum_scatter(grad_query_w, "col", scatter_dimension=0, tiled=True),
        lax.psum_scatter(grad_key_w, "col", scatter_dimension=0, tiled=True),
        lax.psum_scatter(grad_value_w, "col", scatter_dimension=0, tiled=True),
        lax.psum_scatter(grad_out_w, "col", scatter_dimension=1, tiled=True),
        lax.psum_scatter(grad_gate_w, "col", scatter_dimension=0, tiled=True),
        lax.psum_scatter(grad_up_w, "col", scatter_dimension=0, tiled=True),
        lax.psum_scatter(grad_down_w, "col", scatter_dimension=1, tiled=True),
        lax.psum_scatter(tile_attn, "col", scatter_dimension=0, tiled=True),
        lax.psum_scatter(tile_mlp, "col", scatter_dimension=0, tiled=True),
    )
    summed = lax.psum(
        (
            col_summed[0],
            col_summed[1],
            col_summed[2],
            col_summed[3],
            col_summed[4],
            col_summed[5],
            col_summed[6],
            col_summed[7],
            col_summed[8],
        ),
        "dp",
    )
    return (
        result,
        grad_input,
        summed[0],
        summed[1],
        summed[2],
        summed[3],
        summed[4],
        summed[5],
        summed[6],
        summed[7][0],
        summed[8][0],
    )


def solution(mesh):
    placed = (
        P(("dp", "col"), "row"),
        P(("dp", "col"), None),
        P(("dp", "col"), "row"),
        P("col", "row"),
        P("col", "row"),
        P("col", "row"),
        P("row", "col"),
        P("col", "row"),
        P("col", "row"),
        P("row", "col"),
        P("row"),
        P("row"),
    )
    return jax.shard_map(
        per_device,
        mesh=mesh,
        in_specs=placed,
        out_specs=(
            P(("dp", "col"), "row"),
            P(("dp", "col"), "row"),
            P("col", "row"),
            P("col", "row"),
            P("col", "row"),
            P("row", "col"),
            P("col", "row"),
            P("col", "row"),
            P("row", "col"),
            P("row"),
            P("row"),
        ),
        check_vma=False,
    )
```

profile of v0, /device:TPU:0, one launch (start us, length us, event | category | flops | bytes accessed | tf_op | source)
XLA Modules:
  0.0 3193.4 jit_solution(8351349479691408732)
XLA Ops:
  52.6 123.6 %all-gather.10.cloned.1.call-done = bf16[2048,2048]{1,0:T(8,128)(2,1)} async-done(((bf16[2048,512]{1,0:T(8,128)(2,1)}), bf16[2048,2048]{1,0:T(8,128)(2,1)}) %all-gather.10.cloned.1.call-update) | async-done | bytes 8388624 | tf_op jit(solution)/shard_map/all_gather | solution.py:25
  182.6 28.9 all-gather.12.cloned.1.call-done
  228.1 190.7 %while.47 = (s32[]{:T(128)}, bf16[4,512,2,4,64]{1,4,3,2,0:T(8,128)(2,1)}, f32[4,2,4,512]{3,2,1,0:T(4,128)}, s32[4]{0:T(128)S(1)}, s32[2048]{0:T(1024)S(1)}, /*in...) while((s32[]{:T(128)}, ...), condition=%wide.region_7.8_spmd, body=%wide.region_4.7_spmd.sunk | while | flops 2251551232 | bytes 107104456 | solution.py:101
  437.9 280.1 %reduce-scatter.12.cloned.1.call-done = f32[2048,512]{1,0:T(8,128)} async-done(((f32[2048,2048]{1,0:T(8,128)}), f32[2048,512]{1,0:T(8,128)}) %reduce-scatter.12.cloned.1.call-update) | async-done | bytes 4194320 | tf_op jit(solution)/shard_map/reduce_scatter | solution.py:29
  745.8 62.4 %all-gather.20.cloned.1.call-done = bf16[2048,2048]{1,0:T(8,128)(2,1)} async-done(((bf16[512,2048]{1,0:T(8,128)(2,1)}), bf16[2048,2048]{1,0:T(8,128)(2,1)}) %all-gather.20.cloned.1.call-update) | async-done | bytes 8388624 | tf_op jit(solution)/shard_map/all_gather | solution.py:165
  808.2 151.7 %all-gather.16.cloned.1.call-done = bf16[2048,2048]{1,0:T(8,128)(2,1)} async-done(((bf16[2048,512]{1,0:T(8,128)(2,1)}), bf16[2048,2048]{1,0:T(8,128)(2,1)}) %all-gather.16.cloned.1.call-update) | async-done | bytes 8388624 | tf_op jit(solution)/shard_map/all_gather | solution.py:25
  960.0 24.3 fusion.58
  984.3 63.5 %all-gather.18.cloned.1.call-done = bf16[2048,2048]{1,0:T(8,128)(2,1)} async-done(((bf16[512,2048]{1,0:T(8,128)(2,1)}), bf16[2048,2048]{1,0:T(8,128)(2,1)}) %all-gather.18.cloned.1.call-update) | async-done | bytes 8388624 | tf_op jit(solution)/shard_map/all_gather | solution.py:164
  1071.9 65.3 %all-gather.22.cloned.1.call-done = bf16[2048,2048]{1,0:T(8,128)(2,1)} async-done(((bf16[2048,512]{1,0:T(8,128)(2,1)}), bf16[2048,2048]{1,0:T(8,128)(2,1)}) %all-gather.22.cloned.1.call-update) | async-done | bytes 8388624 | tf_op jit(solution)/shard_map/all_gather | solution.py:166
  1137.2 151.9 %all-gather.24.cloned.1.call-done = bf16[2048,2048]{1,0:T(8,128)(2,1)} async-done(((bf16[2048,512]{1,0:T(8,128)(2,1)}), bf16[2048,2048]{1,0:T(8,128)(2,1)}) %all-gather.24.cloned.1.call-update) | async-done | bytes 8388624 | tf_op jit(solution)/shard_map/all_gather | solution.py:25
  1289.2 36.9 %multiply_convert_fusion = (bf16[2048,2048]{1,0:T(8,128)(2,1)}, bf16[2048,2048]{1,0:T(8,128)(2,1)}, bf16[2048,2048]{1,0:T(8,128)(2,1)}) fusion(f32[2048,2048]{1,0:T(8,128)} %fusion.57, f32[2048,2048]{1,0:T(8,128)} %fusion.58, bf16[2048,2048]{1,0:T(8,128)(2,1)} %all-gather.24.cloned.1.call-done, bf16[2048,2048]{1,0:T(8,128)(2,1)} %all-gather.22.cloned.1.call-done), kind=kOutput, calls=%fused_computation.61 | convolution fusion | flops 17246978048 | bytes 75497472 | tf_op jit(solution)/shard_map/td,fd->tf/dot_general | solution.py:211
  1326.0 24.3 fusion.60
  1350.3 26.5 convolution_add_fusion
  1376.9 24.2 fusion.59
  1401.1 254.3 %reduce-scatter.16.cloned.1.call-done = f32[2048,512]{1,0:T(8,128)} async-done(((f32[2048,2048]{1,0:T(8,128)}), f32[2048,512]{1,0:T(8,128)}) %reduce-scatter.16.cloned.1.call-update) | async-done | bytes 4194320 | tf_op jit(solution)/shard_map/reduce_scatter | solution.py:29
  1671.7 267.4 %reduce-scatter.14.cloned.1.call-done = f32[2048,512]{1,0:T(8,128)} async-done(((f32[2048,2048]{1,0:T(8,128)}), f32[2048,512]{1,0:T(8,128)}) %reduce-scatter.14.cloned.1.call-update) | async-done | bytes 4194320 | tf_op jit(solution)/shard_map/reduce_scatter | solution.py:29
  1949.7 24.5 fusion.67
  1974.4 24.4 fusion.68
  1998.8 24.9 fusion.69
  2023.8 76.5 %all-gather.26.cloned.1.call-done = bf16[2048,2048]{1,0:T(8,128)(2,1)} async-done(((bf16[2048,512]{1,0:T(8,128)(2,1)}), bf16[2048,2048]{1,0:T(8,128)(2,1)}) %all-gather.26.cloned.1.call-update) | async-done | bytes 8388624 | tf_op jit(solution)/shard_map/all_gather | solution.py:25
  2124.7 522.8 %while.48 = (s32[]{:T(128)}, f32[2048,2,64]{0,2,1:T(8,128)S(1)}, f32[2048,2,64]{0,2,1:T(8,128)}, f32[4,512,2,4,64]{1,0,4,3,2:T(4,128)}, s32[4]{0:T(128)S(1)}, /*...) while((s32[]{:T(128)}, f32[2048,2,64]{0,2,1:T(8,128)S(1)}, ...), condition=%wide.region_17.18_spmd.clone, body=%wide.region_15.17_spmd.clone.sunk | while | flops 5499253248 | bytes 352979296 | solution.py:139
  2162.4 24.9 fusion.147
  2187.3 29.1 fusion.148
  2293.2 24.9 fusion.147
  2318.1 30.1 fusion.148
  2423.7 24.6 fusion.147
  2448.3 29.9 fusion.148
  2555.8 24.6 fusion.147
  2580.4 27.8 fusion.148
  2729.1 41.8 %reduce-scatter.26.cloned.1.call-done = f32[512,512]{1,0:T(8,128)} async-done(((f32[512,2048]{1,0:T(8,128)}), f32[512,512]{1,0:T(8,128)}) %reduce-scatter.26.cloned.1.call-update) | async-done | bytes 1048592 | tf_op jit(solution)/shard_map/reduce_scatter | solution.py:270
  2770.9 56.3 %reduce-scatter.20.cloned.1.call-done = f32[512,512]{1,0:T(8,128)} async-done(((f32[2048,512]{1,0:T(8,128)}), f32[512,512]{1,0:T(8,128)}) %reduce-scatter.20.cloned.1.call-update) | async-done | bytes 1048592 | tf_op jit(solution)/shard_map/reduce_scatter | solution.py:267
  2827.8 282.0 %reduce-scatter.18.cloned.1.call-done = f32[2048,512]{1,0:T(8,128)} async-done(((f32[2048,2048]{1,0:T(8,128)}), f32[2048,512]{1,0:T(8,128)}) %reduce-scatter.18.cloned.1.call-update) | async-done | bytes 4194320 | tf_op jit(solution)/shard_map/reduce_scatter | solution.py:29
  (288 shorter events, 840.0 us)
Async XLA Ops:
  7.2 168.9 %all-gather.10.cloned.1.call-start = ((), (), s32[]{:S(2)}) async-start(), calls=%async_computation.11 | async-start | bytes 10485760 | tf_op jit(solution)/shard_map/all_gather | solution.py:25
  28.1 183.4 %all-gather.12.cloned.1.call-start = ((), (), s32[]{:S(2)}) async-start(), calls=%async_computation.12 | async-start | bytes 2621440 | tf_op jit(solution)/shard_map/all_gather | solution.py:160
  28.9 395.8 %all-gather.14.cloned.1.call-start = ((), (), s32[]{:S(2)}) async-start(), calls=%async_computation.13 | async-start | bytes 2621440 | tf_op jit(solution)/shard_map/all_gather | solution.py:163
  29.6 688.3 %reduce-scatter.12.cloned.1.call-start = ((), (), s32[]{:S(2)}) async-start(), calls=%async_computation.14 | async-start | bytes 20971520 | tf_op jit(solution)/shard_map/reduce_scatter | solution.py:29
  42.0 140.6 %copy-start.7 = (bf16[2048,128]{1,0:T(8,128)(2,1)}, bf16[2048,128]{1,0:T(8,128)(2,1)S(1)}, u32[]{:S(2)}) copy-start(bf16[2048,128]{1,0:T(8,128)(2,1)S(1)} %all_gather.35) | copy-start | bytes 1572868
  50.8 170.0 %copy-start.5 = (bf16[2048,128]{1,0:T(8,128)(2,1)}, bf16[2048,128]{1,0:T(8,128)(2,1)S(1)}, u32[]{:S(2)}) copy-start(bf16[2048,128]{1,0:T(8,128)(2,1)S(1)} %all_gather.36) | copy-start | bytes 1572868
  52.6 166.6 %copy-start.3 = (f32[2048,32]{0,1:T(8,128)}, f32[2048,32]{0,1:T(8,128)S(1)}, u32[]{:S(2)}) copy-start(f32[2048,32]{0,1:T(8,128)S(1)} %get-tuple-element.313) | copy-start | bytes 786436
  437.2 299.2 %copy-start.26 = (f32[512]{0:T(512)S(1)}, f32[512]{0:T(512)}, u32[]{:S(2)}) copy-start(f32[512]{0:T(512)} %param.27) | copy-start | bytes 6148
  437.2 371.0 %all-gather.20.cloned.1.call-start = ((), (), s32[]{:S(2)}) async-start(), calls=%async_computation.17 | async-start | bytes 10485760 | tf_op jit(solution)/shard_map/all_gather | solution.py:165
  437.8 522.1 %all-gather.16.cloned.1.call-start = ((), (), s32[]{:S(2)}) async-start(), calls=%async_computation.15 | async-start | bytes 10485760 | tf_op jit(solution)/shard_map/all_gather | solution.py:25
  740.4 307.4 %all-gather.18.cloned.1.call-start = ((), (), s32[]{:S(2)}) async-start(), calls=%async_computation.16 | async-start | bytes 10485760 | tf_op jit(solution)/shard_map/all_gather | solution.py:164
  741.2 396.1 %all-gather.22.cloned.1.call-start = ((), (), s32[]{:S(2)}) async-start(), calls=%async_computation.18 | async-start | bytes 10485760 | tf_op jit(solution)/shard_map/all_gather | solution.py:166
  741.9 547.2 %all-gather.24.cloned.1.call-start = ((), (), s32[]{:S(2)}) async-start(), calls=%async_computation.20 | async-start | bytes 10485760 | tf_op jit(solution)/shard_map/all_gather | solution.py:25
  745.8 909.7 %reduce-scatter.16.cloned.1.call-start = ((), (), s32[]{:S(2)}) async-start(), calls=%async_computation.21 | async-start | bytes 20971520 | tf_op jit(solution)/shard_map/reduce_scatter | solution.py:29
  1376.8 562.2 %reduce-scatter.14.cloned.1.call-start = ((), (), s32[]{:S(2)}) async-start(), calls=%async_computation.19 | async-start | bytes 20971520 | tf_op jit(solution)/shard_map/reduce_scatter | solution.py:29
  1401.1 254.4 %copy-start.23 = (f32[2048]{0:T(1024)S(1)}, f32[2048]{0:T(1024)}, u32[]{:S(2)}) copy-start(f32[2048]{0:T(1024)} %copy-done.22) | copy-start | bytes 24580
  1401.1 254.4 %copy-start.27 = (f32[512]{0:T(512)S(1)}, f32[512]{0:T(512)}, u32[]{:S(2)}) copy-start(f32[512]{0:T(512)} %param.27) | copy-start | bytes 6148
  1401.1 538.0 %copy-start.25 = (f32[2048]{0:T(1024)S(1)}, f32[2048]{0:T(1024)}, u32[]{:S(2)}) copy-start(f32[2048]{0:T(1024)} %get-tuple-element.316) | copy-start | bytes 24580
  1401.1 699.2 %all-gather.26.cloned.1.call-start = ((), (), s32[]{:S(2)}) async-start(), calls=%async_computation.22 | async-start | bytes 10485760 | tf_op jit(solution)/shard_map/all_gather | solution.py:25
  1949.7 779.3 %reduce-scatter.28.cloned.1.call-start = ((), (), s32[]{:S(2)}) async-start(), calls=%async_computation.28 | async-start | bytes 20971520 | tf_op jit(solution)/shard_map/reduce_scatter | solution.py:271
  1974.3 754.7 %reduce-scatter.30.cloned.1.call-start = ((), (), s32[]{:S(2)}) async-start(), calls=%async_computation.29 | async-start | bytes 20971520 | tf_op jit(solution)/shard_map/reduce_scatter | solution.py:272
  1998.7 730.3 %reduce-scatter.32.cloned.1.call-start = ((), (), s32[]{:S(2)}) async-start(), calls=%async_computation.30 | async-start | bytes 20971520 | tf_op jit(solution)/shard_map/reduce_scatter | solution.py:273
  2023.7 705.4 %reduce-scatter.24.cloned.1.call-start = ((), (), s32[]{:S(2)}) async-start(), calls=%async_computation.26 | async-start | bytes 1310720 | tf_op jit(solution)/shard_map/reduce_scatter | solution.py:269
  2655.7 73.4 %reduce-scatter.22.cloned.1.call-start = ((), (), s32[]{:S(2)}) async-start(), calls=%async_computation.25 | async-start | bytes 1310720 | tf_op jit(solution)/shard_map/reduce_scatter | solution.py:268
  2662.7 108.2 %reduce-scatter.26.cloned.1.call-start = ((), (), s32[]{:S(2)}) async-start(), calls=%async_computation.27 | async-start | bytes 5242880 | tf_op jit(solution)/shard_map/reduce_scatter | solution.py:270
  2673.4 153.9 %reduce-scatter.20.cloned.1.call-start = ((), (), s32[]{:S(2)}) async-start(), calls=%async_computation.24 | async-start | bytes 5242880 | tf_op jit(solution)/shard_map/reduce_scatter | solution.py:267
  2693.9 415.9 %reduce-scatter.18.cloned.1.call-start = ((), (), s32[]{:S(2)}) async-start(), calls=%async_computation.23 | async-start | bytes 20971520 | tf_op jit(solution)/shard_map/reduce_scatter | solution.py:29
  2728.9 380.9 %copy-start.21 = (f32[2048]{0:T(1024)S(1)}, f32[2048]{0:T(1024)}, u32[]{:S(2)}) copy-start(f32[2048]{0:T(1024)} %copy-done.20) | copy-start | bytes 24580
  2728.9 380.9 %copy-start.28 = (f32[512]{0:T(512)S(1)}, f32[512]{0:T(512)}, u32[]{:S(2)}) copy-start(f32[512]{0:T(512)} %param.26) | copy-start | bytes 6148
  2729.0 440.5 %all-reduce.7.cloned.1.call-start = ((), (), s32[]{:S(2)}) async-start(), calls=%async_computation.31 | async-start | bytes 30408704 | tf_op jit(solution)/shard_map/psum | solution.py:277
  2827.2 286.7 %copy-start.29 = (f32[512]{0:T(512)S(1)}, f32[512]{0:T(512)}, u32[]{:S(2)}) copy-start(f32[512]{0:T(512)} %get-tuple-element.238) | copy-start | bytes 6148
  2827.2 318.0 %copy-start.24 = (f32[2048]{0:T(1024)S(1)}, f32[2048]{0:T(1024)}, u32[]{:S(2)}) copy-start(f32[2048]{0:T(1024)} %get-tuple-element.314) | copy-start | bytes 24580
  (33 other events, 579.9 us)
Sparse Core Ops, SparseCore 0:
  28.3 147.8 all-gather.9
  178.0 33.4 all-gather.11
  213.4 35.1 all-gather.13
  437.3 280.6 reduce-scatter.11
  719.8 88.3 all-gather.19
  810.3 149.6 all-gather.15
  961.9 85.7 all-gather.17
  1049.7 87.4 all-gather.21
  1139.5 149.6 all-gather.23
  1377.0 278.4 reduce-scatter.15
  1657.8 281.1 reduce-scatter.13
  1949.8 150.4 all-gather.25
  2103.6 152.0 reduce-scatter.27
  2258.9 153.7 reduce-scatter.29
  2416.0 153.8 reduce-scatter.31
  2655.8 27.6 reduce-scatter.23
  2686.8 27.7 reduce-scatter.21
  2718.2 52.6 reduce-scatter.25
  2774.5 52.6 reduce-scatter.19
  2829.5 280.2 reduce-scatter.17
  3113.2 56.2 all-reduce.6
where the time goes:
time: 3210 us; the launch traced here: 3190 us
  waiting for transfers between devices  1920 us (60%)
  matrix products  762 us (24%)
  other arithmetic  246 us (8%)
  local copies, waits for them, and re-layouts  151 us (5%)
  blocking collectives  87.3 us (3%)
    reduce_scatter x4, waiting for transfers between devices, reduce_features(): return lax.psum_scatter(values, 'row', scatter_dimension=1, tiled=True)  1080 us
    all_gather x4, waiting for transfers between devices, gather_features(): return lax.all_gather(values, 'row', axis=1, tiled=True)  504 us
    dot_general x8, matrix products, block_scores(): jnp.einsum('qkgd,tkd->kgqt', block_query, keys_rot, preferred_element_typ...  131 us
    convert_element_type x4, other arithmetic, one_block(): grad_scores = (probs_full * (grad_probs - row_delta)).astype(jnp.bfloat16)  117 us
    dot_general x4, matrix products, one_block(): jnp.einsum('qkgd,tkd->kgqt', block_grad, values_low, preferred_element_ty...  99 us
    dynamic_update_slice x8, local copies, waits for them, and re-layouts, attend_backward(): lax.scan(one_block, (empty, empty), (jnp.arange(blocks, dtype=jnp.int32),...  88.8 us
    all_gather x1, waiting for transfers between devices, per_device(): lax.all_gather(w_down, 'col', axis=1, tiled=True)  65.3 us
  transfers between devices with their start and end apart: 21, of which 15 were waited for; matrix products, arithmetic and copies ran while one was open for 32% of the time, Pallas kernels for 0%

commit v1 on v0

v1 whole, which is shorter than its diff:
```python
import functools
import math

import jax
import jax.numpy as jnp
from jax import lax
from jax.experimental import pallas as pl
from jax.experimental.pallas import tpu as pltpu
from jax.sharding import PartitionSpec as P

D = 2048
HEADS = 32
KV = 8
HD = 64
HALF = HD // 2
GROUP = HEADS // KV
BLOCK = 256
ROPE_ROWS = 512

NORM_EPS = 1e-05
ROPE_BASE = 500000.0
MASK_FILL = -1e30
SCORE_SCALE = 1.0 / math.sqrt(HD)
VMEM_BYTES = 40 * 1024 * 1024

NT = (((1,), (1,)), ((), ()))
TN = (((0,), (0,)), ((), ()))
NN = (((1,), (0,)), ((), ()))


def mm(left, right, dims):
    return lax.dot_general(left, right, dims, preferred_element_type=jnp.float32)


def feature_sum(values):
    return lax.psum(values, "row")


def gather_features(values):
    return lax.all_gather(values, "row", axis=1, tiled=True)


def reduce_features(values):
    return lax.psum_scatter(
        values.astype(jnp.bfloat16), "row", scatter_dimension=1, tiled=True
    ).astype(jnp.float32)


def swap_with(values, name, distance):
    pairs = [(i, i ^ distance) for i in range(lax.axis_size(name))]
    return lax.ppermute(values, name, pairs)


def gather_blocks(block, name, axis):
    count, here, size = lax.axis_size(name), lax.axis_index(name), block.shape[axis]
    shape = list(block.shape)
    shape[axis] = size * count
    full = jnp.zeros(shape, block.dtype)
    for distance in range(count):
        piece = swap_with(block, name, distance) if distance else block
        full = lax.dynamic_update_slice_in_dim(full, piece, (here ^ distance) * size, axis)
    return full


def sum_blocks(values, name, axis):
    count, here = lax.axis_size(name), lax.axis_index(name)
    size = values.shape[axis] // count
    total = lax.dynamic_slice_in_dim(values, here * size, size, axis).astype(jnp.float32)
    for distance in range(1, count):
        piece = lax.dynamic_slice_in_dim(values, (here ^ distance) * size, size, axis)
        total = total + swap_with(piece, name, distance).astype(jnp.float32)
    return total.astype(jnp.bfloat16)


def gather_weight(weight, axis):
    return gather_blocks(weight, "col", axis)


def reduce_weight(grad, axis):
    half = sum_blocks(grad.astype(jnp.bfloat16), "dp", 1 - axis)
    part = sum_blocks(half, "col", axis)
    return gather_blocks(part, "dp", 1 - axis).astype(jnp.float32)


def doc_starts(segment_row):
    token_ids = jnp.arange(segment_row.shape[0], dtype=jnp.int32)
    starts = jnp.concatenate([jnp.ones((1,), dtype=jnp.bool_), segment_row[1:] != segment_row[:-1]])
    return lax.cummax(jnp.where(starts, token_ids, 0), axis=0)


def rope_tables(places):
    inverse = ROPE_BASE ** (-jnp.arange(HALF, dtype=jnp.float32) * 2.0 / HD)
    angles = places.astype(jnp.float32)[:, None] * inverse[None, :]
    return (jnp.cos(angles), jnp.sin(angles))


def norm_forward(tokens_in, gain_row):
    totals = feature_sum(jnp.sum(tokens_in * tokens_in, axis=1))
    scale_rows = lax.rsqrt(totals / D + NORM_EPS)[:, None]
    return (scale_rows, (tokens_in * scale_rows * gain_row).astype(jnp.bfloat16))


def norm_backward(tokens_in, scale_rows, gain_row, grad_normed):
    inner_sum = feature_sum(jnp.sum(grad_normed * gain_row * tokens_in, axis=1))[:, None]
    grad_in = scale_rows * gain_row * grad_normed - tokens_in * scale_rows**3 * inner_sum / D
    grad_gain = jnp.sum(grad_normed * tokens_in * scale_rows, axis=0)
    return (grad_in, grad_gain)


def rope_kernel(heads, kv, raw_ref, cos_ref, sin_ref, q_ref, k_ref, v_ref):
    cosine, sine_part = cos_ref[...], sin_ref[...]
    for h in range(heads + kv):
        first = raw_ref[:, h * HD : h * HD + HALF]
        second = raw_ref[:, h * HD + HALF : (h + 1) * HD]
        rot = jnp.concatenate(
            [first * cosine - second * sine_part, second * cosine + first * sine_part], axis=1
        )
        if h < heads:
            q_ref[h] = (rot * SCORE_SCALE).astype(jnp.bfloat16)
        else:
            k_ref[h - heads] = rot.astype(jnp.bfloat16)
    for h in range(kv):
        at = (heads + kv + h) * HD
        v_ref[h] = raw_ref[:, at : at + HD].astype(jnp.bfloat16)


def rope_split(raw, cosine, sine_part, heads, kv):
    rows = raw.shape[0]
    return pl.pallas_call(
        functools.partial(rope_kernel, heads, kv),
        grid=(rows // ROPE_ROWS,),
        in_specs=[
            pl.BlockSpec((ROPE_ROWS, raw.shape[1]), lambda i: (i, 0)),
            pl.BlockSpec((ROPE_ROWS, HALF), lambda i: (i, 0)),
            pl.BlockSpec((ROPE_ROWS, HALF), lambda i: (i, 0)),
        ],
        out_specs=[
            pl.BlockSpec((heads, ROPE_ROWS, HD), lambda i: (0, i, 0)),
            pl.BlockSpec((kv, ROPE_ROWS, HD), lambda i: (0, i, 0)),
            pl.BlockSpec((kv, ROPE_ROWS, HD), lambda i: (0, i, 0)),
        ],
        out_shape=[
            jax.ShapeDtypeStruct((heads, rows, HD), jnp.bfloat16),
            jax.ShapeDtypeStruct((kv, rows, HD), jnp.bfloat16),
            jax.ShapeDtypeStruct((kv, rows, HD), jnp.bfloat16),
        ],
        compiler_params=pltpu.CompilerParams(vmem_limit_bytes=VMEM_BYTES),
        name="rope_split",
    )(raw, cosine, sine_part)


def block_mask(block_at, starts, query_block):
    wide = GROUP * BLOCK
    lane = lax.broadcasted_iota(jnp.int32, (1, wide), 1)
    query_ids = query_block * BLOCK + lax.rem(lane, BLOCK)
    key_ids = block_at * BLOCK + lax.broadcasted_iota(jnp.int32, (BLOCK, wide), 0)
    return (key_ids <= query_ids) & (key_ids >= starts)


def attend_kernel(first_ref, q_ref, k_ref, v_ref, start_ref, o_ref, lse_ref):
    seq, query_block = pl.program_id(0), pl.program_id(2)
    blocks = pl.num_programs(2)
    wide = GROUP * BLOCK
    queries = q_ref[...].reshape(wide, HD)
    starts = jnp.concatenate([start_ref[0]] * GROUP, axis=1)

    def step(at, carry):
        top, total, acc = carry
        rows = pl.ds(pl.multiple_of(at * BLOCK, BLOCK), BLOCK)
        scores = mm(k_ref[0, rows, :], queries, NT)
        scores = jnp.where(block_mask(at, starts, query_block), scores, MASK_FILL)
        new_top = jnp.maximum(top, jnp.max(scores, axis=0, keepdims=True))
        probs = jnp.exp(scores - new_top)
        shrink = jnp.exp(top - new_top)
        total = total * shrink + jnp.sum(probs, axis=0, keepdims=True)
        acc = acc * shrink + mm(v_ref[0, rows, :], probs.astype(jnp.bfloat16), TN)
        return (new_top, total, acc)

    empty = (
        jnp.full((1, wide), MASK_FILL, jnp.float32),
        jnp.zeros((1, wide), jnp.float32),
        jnp.zeros((HD, wide), jnp.float32),
    )
    top, total, acc = lax.fori_loop(
        first_ref[seq * blocks + query_block], query_block + 1, step, empty
    )
    mixed = acc / total
    o_ref[...] = jnp.concatenate(
        [mixed[:, h * BLOCK : (h + 1) * BLOCK].T for h in range(GROUP)], axis=1
    ).astype(jnp.bfloat16)
    lse_ref[0] = top + jnp.log(total)


def attend_forward(first, queries, keys, values, starts, seqs):
    heads, rows, _ = queries.shape
    kv = keys.shape[0]
    length = rows // seqs
    blocks = length // BLOCK
    wide = GROUP * BLOCK
    return pl.pallas_call(
        attend_kernel,
        grid_spec=pltpu.PrefetchScalarGridSpec(
            num_scalar_prefetch=1,
            grid=(seqs, kv, blocks),
            in_specs=[
                pl.BlockSpec((GROUP, BLOCK, HD), lambda s, k, b, f: (k, s * blocks + b, 0)),
                pl.BlockSpec((1, length, HD), lambda s, k, b, f: (k, s, 0)),
                pl.BlockSpec((1, length, HD), lambda s, k, b, f: (k, s, 0)),
                pl.BlockSpec((1, 1, BLOCK), lambda s, k, b, f: (s, 0, b)),
            ],
            out_specs=[
                pl.BlockSpec((BLOCK, GROUP * HD), lambda s, k, b, f: (s * blocks + b, k)),
                pl.BlockSpec((1, 1, wide), lambda s, k, b, f: (k, 0, s * blocks + b)),
            ],
        ),
        out_shape=[
            jax.ShapeDtypeStruct((rows, heads * HD), jnp.bfloat16),
            jax.ShapeDtypeStruct((kv, 1, rows * GROUP), jnp.float32),
        ],
        compiler_params=pltpu.CompilerParams(vmem_limit_bytes=VMEM_BYTES),
        name="attend_forward",
    )(first, queries, keys, values, starts)


def split_heads(block):
    return jnp.concatenate([block[:, h * HD : (h + 1) * HD] for h in range(GROUP)], axis=0)


def grads_kernel(
    first_ref, q_ref, k_ref, v_ref, start_ref, lse_ref, mixed_ref, grad_ref,
    cos_ref, sin_ref, cos_t_ref, sin_t_ref, dq_ref, dk_ref, dv_ref, key_acc, value_acc,
):
    seq, query_block = pl.program_id(0), pl.program_id(2)
    blocks = pl.num_programs(2)
    wide = GROUP * BLOCK

    @pl.when(query_block == 0)
    def _():
        key_acc[...] = jnp.zeros_like(key_acc)
        value_acc[...] = jnp.zeros_like(value_acc)

    queries = q_ref[...].reshape(wide, HD)
    grads = split_heads(grad_ref[...])
    product = grads.astype(jnp.float32) * split_heads(mixed_ref[...]).astype(jnp.float32)
    delta = jnp.sum(product.T, axis=0, keepdims=True)
    log_sums = lse_ref[0]
    starts = jnp.concatenate([start_ref[0]] * GROUP, axis=1)

    def step(at, acc):
        rows = pl.ds(pl.multiple_of(at * BLOCK, BLOCK), BLOCK)
        keys = k_ref[0, rows, :]
        scores = mm(keys, queries, NT)
        scores = jnp.where(block_mask(at, starts, query_block), scores, MASK_FILL)
        probs = jnp.exp(scores - log_sums)
        grad_probs = mm(v_ref[0, rows, :], grads, NT)
        grad_scores = (probs * (grad_probs - delta)).astype(jnp.bfloat16)
        value_acc[rows, :] += mm(probs.astype(jnp.bfloat16), grads, NN)
        key_acc[rows, :] += mm(grad_scores, queries, NN)
        return acc + mm(keys, grad_scores, TN)

    acc = lax.fori_loop(
        first_ref[seq * blocks + query_block],
        query_block + 1,
        step,
        jnp.zeros((HD, wide), jnp.float32),
    )
    cosine, sine_part = cos_t_ref[...], sin_t_ref[...]
    pieces = []
    for h in range(GROUP):
        head = acc[:, h * BLOCK : (h + 1) * BLOCK] * SCORE_SCALE
        top, low = head[:HALF], head[HALF:]
        turned = jnp.concatenate(
            [top * cosine + low * sine_part, low * cosine - top * sine_part], axis=0
        )
        pieces.append(turned.T)
    dq_ref[...] = jnp.concatenate(pieces, axis=1).astype(jnp.bfloat16)

    @pl.when(query_block == blocks - 1)
    def _():
        cosine, sine_part = cos_ref[...], sin_ref[...]
        first, second = key_acc[:, :HALF], key_acc[:, HALF:]
        dk_ref[0] = jnp.concatenate(
            [first * cosine + second * sine_part, second * cosine - first * sine_part], axis=1
        ).astype(jnp.bfloat16)
        dv_ref[0] = value_acc[...].astype(jnp.bfloat16)


def attend_backward(
    first, queries, keys, values, starts, log_sums, mixed, grad_mixed, cosine, sine_part, seqs
):
    heads, rows, _ = queries.shape
    kv = keys.shape[0]
    length = rows // seqs
    blocks = length // BLOCK
    wide = GROUP * BLOCK
    return pl.pallas_call(
        grads_kernel,
        grid_spec=pltpu.PrefetchScalarGridSpec(
            num_scalar_prefetch=1,
            grid=(seqs, kv, blocks),
            in_specs=[
                pl.BlockSpec((GROUP, BLOCK, HD), lambda s, k, b, f: (k, s * blocks + b, 0)),
                pl.BlockSpec((1, length, HD), lambda s, k, b, f: (k, s, 0)),
                pl.BlockSpec((1, length, HD), lambda s, k, b, f: (k, s, 0)),
                pl.BlockSpec((1, 1, BLOCK), lambda s, k, b, f: (s, 0, b)),
                pl.BlockSpec((1, 1, wide), lambda s, k, b, f: (k, 0, s * blocks + b)),
                pl.BlockSpec((BLOCK, GROUP * HD), lambda s, k, b, f: (s * blocks + b, k)),
                pl.BlockSpec((BLOCK, GROUP * HD), lambda s, k, b, f: (s * blocks + b, k)),
                pl.BlockSpec((length, HALF), lambda s, k, b, f: (s, 0)),
                pl.BlockSpec((length, HALF), lambda s, k, b, f: (s, 0)),
                pl.BlockSpec((HALF, BLOCK), lambda s, k, b, f: (0, s * blocks + b)),
                pl.BlockSpec((HALF, BLOCK), lambda s, k, b, f: (0, s * blocks + b)),
            ],
            out_specs=[
                pl.BlockSpec((BLOCK, GROUP * HD), lambda s, k, b, f: (s * blocks + b, k)),
                pl.BlockSpec((1, length, HD), lambda s, k, b, f: (k, s, 0)),
                pl.BlockSpec((1, length, HD), lambda s, k, b, f: (k, s, 0)),
            ],
            scratch_shapes=[
                pltpu.VMEM((length, HD), jnp.float32),
                pltpu.VMEM((length, HD), jnp.float32),
            ],
        ),
        out_shape=[
            jax.ShapeDtypeStruct((rows, heads * HD), jnp.bfloat16),
            jax.ShapeDtypeStruct((kv, rows, HD), jnp.bfloat16),
            jax.ShapeDtypeStruct((kv, rows, HD), jnp.bfloat16),
        ],
        compiler_params=pltpu.CompilerParams(vmem_limit_bytes=VMEM_BYTES),
        name="attend_backward",
    )(
        first, queries, keys, values, starts, log_sums, mixed, grad_mixed,
        cosine, sine_part, cosine.T, sine_part.T,
    )


def per_device(
    tokens,
    segments,
    cotangent,
    w_query,
    w_key,
    w_value,
    w_out,
    w_gate,
    w_up,
    w_down,
    gain_attn,
    gain_mlp,
):
    seqs, length = segments.shape
    rows = tokens.shape[0]
    heads = w_query.shape[1] // HD
    kv = w_key.shape[1] // HD
    wide_q, wide_kv = heads * HD, kv * HD

    qkv_full = gather_weight(jnp.concatenate([w_query, w_key, w_value], axis=1), 0)
    out_full = gather_weight(w_out, 1)
    gate_full = gather_weight(w_gate, 0)
    up_full = gather_weight(w_up, 0)
    down_full = gather_weight(w_down, 1)

    starts = jax.vmap(doc_starts)(segments)
    places = (jnp.arange(length, dtype=jnp.int32)[None, :] - starts).reshape(rows)
    cosine, sine_part = rope_tables(places)
    first = (starts[:, ::BLOCK] // BLOCK).reshape(-1)
    starts = starts[:, None, :]

    scale_one, normed_local = norm_forward(tokens, gain_attn)
    normed_one = gather_features(normed_local)
    normed_one, cotangent_low = lax.optimization_barrier(
        (normed_one, cotangent.astype(jnp.bfloat16))
    )
    grad_branch = gather_features(cotangent_low)
    raw = mm(normed_one, qkv_full, NN)
    queries, keys, values = rope_split(raw, cosine, sine_part, heads, kv)
    mixed, log_sums = attend_forward(first, queries, keys, values, starts, seqs)
    attn_part, grad_branch = lax.optimization_barrier(
        (mm(mixed, out_full, NN).astype(jnp.bfloat16), grad_branch)
    )
    after_attn = tokens + reduce_features(attn_part)
    scale_two, normed_local_two = norm_forward(after_attn, gain_mlp)
    normed_two = gather_features(normed_local_two)
    gate_act = mm(normed_two, gate_full, NN)
    up_proj = mm(normed_two, up_full, NN)
    sigmoid_gate = jax.nn.sigmoid(gate_act)
    hidden = (gate_act * sigmoid_gate * up_proj).astype(jnp.bfloat16)
    result = after_attn + reduce_features(mm(hidden, down_full, NN))

    grad_w_down = reduce_weight(mm(hidden, grad_branch, TN), 1)
    grad_hidden = mm(grad_branch, down_full, NT)
    grad_gate = (
        grad_hidden * up_proj * sigmoid_gate * (1.0 + gate_act * (1.0 - sigmoid_gate))
    ).astype(jnp.bfloat16)
    grad_up = (grad_hidden * gate_act * sigmoid_gate).astype(jnp.bfloat16)
    grad_w_gate = reduce_weight(mm(normed_two, grad_gate, TN), 0)
    grad_w_up = reduce_weight(mm(normed_two, grad_up, TN), 0)
    grad_normed_two = reduce_features(mm(grad_gate, gate_full, NT) + mm(grad_up, up_full, NT))
    grad_after, gain_two = norm_backward(after_attn, scale_two, gain_mlp, grad_normed_two)
    grad_after = cotangent + grad_after
    grad_attn_branch = gather_features(grad_after.astype(jnp.bfloat16))
    grad_w_out = reduce_weight(mm(mixed, grad_attn_branch, TN), 1)
    grad_mixed = mm(grad_attn_branch, out_full, NT).astype(jnp.bfloat16)
    grad_query, grad_key, grad_value = attend_backward(
        first, queries, keys, values, starts, log_sums, mixed, grad_mixed, cosine, sine_part, seqs
    )
    grad_key = jnp.swapaxes(grad_key, 0, 1).reshape(rows, wide_kv)
    grad_value = jnp.swapaxes(grad_value, 0, 1).reshape(rows, wide_kv)
    grad_qkv = jnp.concatenate([grad_query, grad_key, grad_value], axis=1)
    grad_normed_one = reduce_features(mm(grad_qkv, qkv_full, NT))
    grad_w_qkv = reduce_weight(mm(normed_one, grad_qkv, TN), 0)
    grad_before, gain_one = norm_backward(tokens, scale_one, gain_attn, grad_normed_one)
    gains = lax.psum(jnp.stack([gain_one, gain_two]), ("dp", "col"))
    return (
        result,
        grad_after + grad_before,
        grad_w_qkv[:, :wide_q],
        grad_w_qkv[:, wide_q : wide_q + wide_kv],
        grad_w_qkv[:, wide_q + wide_kv :],
        grad_w_out,
        grad_w_gate,
        grad_w_up,
        grad_w_down,
        gains[0],
        gains[1],
    )


def solution(mesh):
    placed = (
        P(("dp", "col"), "row"),
        P(("dp", "col"), None),
        P(("dp", "col"), "row"),
        P("col", "row"),
        P("col", "row"),
        P("col", "row"),
        P("row", "col"),
        P("col", "row"),
        P("col", "row"),
        P("row", "col"),
        P("row"),
        P("row"),
    )
    return jax.shard_map(
        per_device,
        mesh=mesh,
        in_specs=placed,
        out_specs=(
            P(("dp", "col"), "row"),
            P(("dp", "col"), "row"),
            P("col", "row"),
            P("col", "row"),
            P("col", "row"),
            P("row", "col"),
            P("col", "row"),
            P("col", "row"),
            P("row", "col"),
            P("row"),
            P("row"),
        ),
        check_vma=False,
    )
```

time: 3210 us -> 1700 us (0.53)
  waiting for transfers between devices: 1920 us -> 1030 us
  matrix products: 762 us -> 282 us
  other arithmetic: 246 us -> 82.3 us
  Pallas kernels: 0 us -> 100 us
  local copies, waits for them, and re-layouts: 151 us -> 79 us
  starting transfers between devices: 0.86 us -> 43.1 us
    reduce_scatter x11 -> x4, waiting for transfers between devices: 1180 us -> 394 us  [reduce_features(): lax.psum_scatter(values.astype(jnp.bfloat16), 'row', scatter_dimension=1,...]
    dot_general x49 -> x15, matrix products: 762 us -> 282 us  [mm(): lax.dot_general(left, right, dims, preferred_element_type=jnp.float32)]
    ppermute x0 -> x40, waiting for transfers between devices: none -> 385 us  [swap_with(): return lax.ppermute(values, name, pairs)]
    all_gather x4, waiting for transfers between devices: 504 us -> 253 us  [gather_features(): return lax.all_gather(values, 'row', axis=1, tiled=True)]
    all_gather x5 -> x0, waiting for transfers between devices: 220 us -> none  [the longest x1 65.3 us: per_device(): lax.all_gather(w_down, 'col', axis=1, tiled=True)]
    pallas_call x0 -> x3, Pallas kernels: none -> 100 us  [the longest x1 53.3 us: attend_backward(): pl.pallas_call(grads_kernel, grid_spec=pltpu.PrefetchScalarGridSpec(num_s...]
    convert_element_type x6 -> x10, other arithmetic: 122 us -> 30.4 us  [the longest x5 17.7 us: sum_blocks(): return total.astype(jnp.bfloat16)]
    reduce_sum x4 -> x0, other arithmetic: 59.9 us -> none  [one_block(): row_total = jnp.sum(exp_scores, axis=-1, keepdims=True)]
  transfers between devices with their start and end apart: 21 -> 48, of which waited for: 15 -> 24; matrix products, arithmetic and copies ran while one was open for 32% -> 17% of each run, Pallas kernels for 0% -> 6%
where the time goes in v1:
time: 1700 us; the launch traced here: 1690 us
  waiting for transfers between devices  1030 us (61%)
  matrix products  282 us (17%)
  Pallas kernels  100 us (6%)
  other arithmetic  82.3 us (5%)
  local copies, waits for them, and re-layouts  79 us (5%)
  blocking collectives  59.6 us (4%)
  starting transfers between devices  43.1 us (3%)
    reduce_scatter x4, waiting for transfers between devices, reduce_features(): lax.psum_scatter(values.astype(jnp.bfloat16), 'row', scatter_dimension=1,...  394 us
    ppermute x40, waiting for transfers between devices, swap_with(): return lax.ppermute(values, name, pairs)  385 us
    dot_general x15, matrix products, mm(): lax.dot_general(left, right, dims, preferred_element_type=jnp.float32)  282 us
    all_gather x4, waiting for transfers between devices, gather_features(): return lax.all_gather(values, 'row', axis=1, tiled=True)  253 us
    pallas_call x1, Pallas kernels, attend_backward(): pl.pallas_call(grads_kernel, grid_spec=pltpu.PrefetchScalarGridSpec(num_s...  53.3 us
    psum x4, blocking collectives, feature_sum(): return lax.psum(values, 'row')  46.1 us
    ppermute x40, starting transfers between devices, swap_with(): return lax.ppermute(values, name, pairs)  42.6 us
    pallas_call x1, Pallas kernels, attend_forward(): pl.pallas_call(attend_kernel, grid_spec=pltpu.PrefetchScalarGridSpec(num_...  35.2 us
  transfers between devices with their start and end apart: 48, of which 24 were waited for; matrix products, arithmetic and copies ran while one was open for 17% of the time, Pallas kernels for 6%

profile of v1, /device:TPU:0, one launch (start us, length us, event | category | flops | bytes accessed | tf_op | source)
XLA Modules:
  0.0 1693.4 jit_solution(14149906299074619515)
XLA Ops:
  9.8 13.7 psum.35
  32.6 144.0 %all-gather.5.cloned.1.call-done = bf16[2048,2048]{1,0:T(8,128)(2,1)} async-done(((bf16[2048,512]{1,0:T(8,128)(2,1)}), bf16[2048,2048]{1,0:T(8,128)(2,1)}) %all-gather.5.cloned.1.call-update) | async-done | bytes 8388624 | tf_op jit(solution)/shard_map/all_gather | solution.py:40
  188.3 20.4 %collective-permute-done.3 = bf16[512,512]{1,0:T(8,128)(2,1)} collective-permute-done((bf16[512,512]{1,0:T(8,128)(2,1)S(1)}, bf16[512,512]{1,0:T(8,128)(2,1)}, u32[]{:S(2)}, u32[]{:S(2)}) %collective-permute-start.3) | collective-permute-done | bytes 524320 | tf_op jit(solution)/shard_map/ppermute | solution.py:51
  215.9 21.2 %collective-permute-done.4 = bf16[512,512]{1,0:T(8,128)(2,1)} collective-permute-done((bf16[512,512]{1,0:T(8,128)(2,1)S(1)}, bf16[512,512]{1,0:T(8,128)(2,1)}, u32[]{:S(2)}, u32[]{:S(2)}) %collective-permute-start.4) | collective-permute-done | bytes 524320 | tf_op jit(solution)/shard_map/ppermute | solution.py:51
  244.6 11.9 fusion.21.raw_ref
  256.4 11.9 rope_split.1
  268.4 35.2 %attend_forward.1 = (bf16[2048,512]{1,0:T(8,128)(2,1)S(1)}, f32[2,1,8192]{2,1,0:T(1,128)S(1)}) custom-call(s32[8]{0:T(128)S(1)} %fusion.14.first_ref, bf16[8,2048,64]{2,1,0:T(8,128)(2,1)S(1)} %get-tuple-element.24.q_ref, bf16[2,2048,64]{2,1,0:T(8,128)(2,1)S(1)} %get-tuple-element.25.k_ref, bf16[2,2048,64]{2,1,0:T(8,128)(2,1)S(1)} %get-tuple-element.26.v_ref, ...), custom_call_target="tpu_custom_call" | custom-call | tf_op jit(solution)/shard_map/attend_forward/pallas_call | solution.py:200
  326.7 145.0 %reduce-scatter.5.cloned.1.call-done = bf16[2048,512]{1,0:T(8,128)(2,1)} async-done(((bf16[2048,2048]{1,0:T(8,128)(2,1)}), bf16[2048,512]{1,0:T(8,128)(2,1)}) %reduce-scatter.5.cloned.1.call-update) | async-done | bytes 2097168 | tf_op jit(solution)/shard_map/reduce_scatter | solution.py:44
  500.6 42.1 %collective-permute-done.9 = bf16[512,2048]{1,0:T(8,128)(2,1)S(1)} collective-permute-done((bf16[512,2048]{1,0:T(8,128)(2,1)}, bf16[512,2048]{1,0:T(8,128)(2,1)S(1)}, u32[]{:S(2)}, u32[]{:S(2)}) %collective-permute-start.9) | collective-permute-done | bytes 2097184 | tf_op jit(solution)/shard_map/ppermute | solution.py:51
  548.0 41.3 %collective-permute-done.10 = bf16[512,2048]{1,0:T(8,128)(2,1)S(1)} collective-permute-done((bf16[512,2048]{1,0:T(8,128)(2,1)}, bf16[512,2048]{1,0:T(8,128)(2,1)S(1)}, u32[]{:S(2)}, u32[]{:S(2)}) %collective-permute-start.10) | collective-permute-done | bytes 2097184 | tf_op jit(solution)/shard_map/ppermute | solution.py:51
  601.9 30.8 %collective-permute-done.12 = bf16[2048,512]{1,0:T(8,128)(2,1)} collective-permute-done((bf16[2048,512]{1,0:T(8,128)(2,1)}, bf16[2048,512]{1,0:T(8,128)(2,1)}, u32[]{:S(2)}, u32[]{:S(2)}) %collective-permute-start.12) | collective-permute-done | bytes 2097184 | tf_op jit(solution)/shard_map/ppermute | solution.py:51
  641.3 38.0 %collective-permute-done.13 = bf16[2048,512]{1,0:T(8,128)(2,1)} collective-permute-done((bf16[2048,512]{1,0:T(8,128)(2,1)}, bf16[2048,512]{1,0:T(8,128)(2,1)}, u32[]{:S(2)}, u32[]{:S(2)}) %collective-permute-start.13) | collective-permute-done | bytes 2097184 | tf_op jit(solution)/shard_map/ppermute | solution.py:51
  683.4 39.3 %collective-permute-done.6 = bf16[512,2048]{1,0:T(8,128)(2,1)} collective-permute-done((bf16[512,2048]{1,0:T(8,128)(2,1)}, bf16[512,2048]{1,0:T(8,128)(2,1)}, u32[]{:S(2)}, u32[]{:S(2)}) %collective-permute-start.6) | collective-permute-done | bytes 2097184 | tf_op jit(solution)/shard_map/ppermute | solution.py:51
  725.8 39.9 %collective-permute-done.7 = bf16[512,2048]{1,0:T(8,128)(2,1)} collective-permute-done((bf16[512,2048]{1,0:T(8,128)(2,1)}, bf16[512,2048]{1,0:T(8,128)(2,1)}, u32[]{:S(2)}, u32[]{:S(2)}) %collective-permute-start.7) | collective-permute-done | bytes 2097184 | tf_op jit(solution)/shard_map/ppermute | solution.py:51
  770.4 20.8 %fusion.23 = f32[2048,2048]{1,0:T(8,128)} fusion(bf16[2048,2048]{1,0:T(8,128)(2,1)S(1)} %bitcast.69, bf16[2048,2048]{1,0:T(8,128)(2,1)S(1)} %constant_dynamic-update-slice_fusion.10), kind=kOutput, calls=%fused_computation.132 | convolution fusion | flops 17179869184 | bytes 33554432 | tf_op jit(solution)/shard_map/dot_general | solution.py:32
  791.2 24.2 %fusion.22 = f32[2048,2048]{1,0:T(8,128)} fusion(bf16[2048,2048]{1,0:T(8,128)(2,1)} %all-gather.9.cloned.1.call-done, bf16[2048,2048]{1,0:T(8,128)(2,1)} %copy-done.19), kind=kOutput, calls=%fused_computation.131 | convolution fusion | flops 17179869184 | bytes 33554432 | tf_op jit(solution)/shard_map/dot_general | solution.py:32
  815.4 36.0 %multiply_convert_fusion.1 = (bf16[2048,2048]{1,0:T(8,128)(2,1)}, bf16[2048,2048]{1,0:T(8,128)(2,1)}, bf16[2048,2048]{1,0:T(8,128)(2,1)}) fusion(f32[2048,2048]{1,0:T(8,128)} %fusion.23, f32[2048,2048]{1,0:T(8,128)} %fusion.22, bf16[2048,2048]{1,0:T(8,128)(2,1)} %all-gather.9.cloned.1.call-done, bf16[2048,2048]{1,0:T(8,128)(2,1)} %constant_dynamic-update-slice_fusion.18), kind=kOutput, calls=%fused_computation.2 | convolution fusion | flops 17246978048 | bytes 75497472 | tf_op jit(solution)/shard_map/dot_general | solution.py:32
  851.5 24.4 %fusion.24 = f32[2048,2048]{1,0:T(8,128)} fusion(bf16[2048,2048]{1,0:T(8,128)(2,1)} %get-tuple-element.55, bf16[2048,2048]{1,0:T(8,128)(2,1)} %copy-done.19), kind=kOutput, calls=%fused_computation.133 | convolution fusion | flops 17179869184 | bytes 33554432 | tf_op jit(solution)/shard_map/dot_general | solution.py:32
  875.8 25.7 %add_convert_fusion = bf16[2048,2048]{1,0:T(8,128)(2,1)} fusion(f32[2048,2048]{1,0:T(8,128)} %fusion.24, bf16[2048,2048]{1,0:T(8,128)(2,1)} %get-tuple-element.53, bf16[2048,2048]{1,0:T(8,128)(2,1)} %constant_dynamic-update-slice_fusion.18), kind=kOutput, calls=%fused_computation | convolution fusion | flops 17188257792 | bytes 41943040 | tf_op jit(solution)/shard_map/dot_general | solution.py:32
  901.6 24.3 %convolution_convert_fusion.4 = bf16[2048,2048]{1,0:T(8,128)(2,1)} fusion(bf16[2048,2048]{1,0:T(8,128)(2,1)} %get-tuple-element.54, bf16[2048,2048]{1,0:T(8,128)(2,1)} %copy-done.20), kind=kOutput, calls=%fused_computation.12 | convolution fusion | flops 17184063488 | bytes 25165824 | tf_op jit(solution)/shard_map/dot_general | solution.py:32
  926.0 117.5 %reduce-scatter.9.cloned.1.call-done = bf16[2048,512]{1,0:T(8,128)(2,1)} async-done(((bf16[2048,2048]{1,0:T(8,128)(2,1)}), bf16[2048,512]{1,0:T(8,128)(2,1)}) %reduce-scatter.9.cloned.1.call-update) | async-done | bytes 2097168 | tf_op jit(solution)/shard_map/reduce_scatter | solution.py:44
  1059.3 131.8 %reduce-scatter.7.cloned.1.call-done = bf16[2048,512]{1,0:T(8,128)(2,1)} async-done(((bf16[2048,2048]{1,0:T(8,128)(2,1)}), bf16[2048,512]{1,0:T(8,128)(2,1)}) %reduce-scatter.7.cloned.1.call-update) | async-done | bytes 2097168 | tf_op jit(solution)/shard_map/reduce_scatter | solution.py:44
  1201.0 22.4 %convolution_convert_fusion = bf16[2048,2048]{1,0:T(8,128)(2,1)S(1)} fusion(bf16[2048,2048]{1,0:T(8,128)(2,1)} %get-tuple-element.54, bf16[2048,2048]{1,0:T(8,128)(2,1)} %all-gather.7.cloned.1.call-done), kind=kOutput, calls=%fused_computation.8 | convolution fusion | flops 17184063488 | bytes 25165824 | tf_op jit(solution)/shard_map/dot_general | solution.py:32
  1228.0 24.3 %convolution_convert_fusion.1 = bf16[2048,2048]{1,0:T(8,128)(2,1)} fusion(bf16[2048,2048]{1,0:T(8,128)(2,1)} %all-gather.9.cloned.1.call-done, bf16[2048,2048]{1,0:T(8,128)(2,1)} %get-tuple-element.55), kind=kOutput, calls=%fused_computation.9 | convolution fusion | flops 17184063488 | bytes 25165824 | tf_op jit(solution)/shard_map/dot_general | solution.py:32
  1252.3 97.2 %all-gather.11.cloned.1.call-done = bf16[2048,2048]{1,0:T(8,128)(2,1)} async-done(((bf16[2048,512]{1,0:T(8,128)(2,1)}), bf16[2048,2048]{1,0:T(8,128)(2,1)}) %all-gather.11.cloned.1.call-update) | async-done | bytes 8388624 | tf_op jit(solution)/shard_map/all_gather | solution.py:40
  1358.3 53.3 %attend_backward.1 = (bf16[2048,512]{1,0:T(8,128)(2,1)S(1)}, bf16[2,2048,64]{2,1,0:T(8,128)(2,1)S(1)}, bf16[2,2048,64]{2,1,0:T(8,128)(2,1)S(1)}) custom-call(s32[8]{0:T(128)S(1)} %copy-done.14, bf16[8,2048,64]{2,1,0:T(8,128)(2,1)} %copy-done, bf16[2,2048,64]{2,1,0:T(8,128)(2,1)S(1)} %copy-done.2, bf16[2,2048,64]{2,1,0:T(8,128)(2,1)S(1)} %copy-done.4, ...), custom_call_target="tpu_custom_call" | custom-call | tf_op jit(solution)/shard_map/attend_backward/pallas_call | solution.py:296
  1434.8 22.6 %convolution_convert_fusion.2 = bf16[2048,2048]{1,0:T(8,128)(2,1)S(1)} fusion(bf16[2048,2048]{1,0:T(8,128)(2,1)} %all-gather.9.cloned.1.call-done, bf16[2048,2048]{1,0:T(8,128)(2,1)} %get-tuple-element.53), kind=kOutput, calls=%fused_computation.10 | convolution fusion | flops 17184063488 | bytes 25165824 | tf_op jit(solution)/shard_map/dot_general | solution.py:32
  1500.8 19.4 %collective-permute-done.37 = bf16[1024,512]{1,0:T(8,128)(2,1)S(1)} collective-permute-done((bf16[1024,512]{1,0:T(8,128)(2,1)}, bf16[1024,512]{1,0:T(8,128)(2,1)S(1)}, u32[]{:S(2)}, u32[]{:S(2)}) %collective-permute-start.37) | collective-permute-done | bytes 1048608 | tf_op jit(solution)/shard_map/ppermute | solution.py:51
  1543.9 21.4 %collective-permute-done.32 = bf16[512,1024]{1,0:T(8,128)(2,1)} collective-permute-done((bf16[512,1024]{1,0:T(8,128)(2,1)}, bf16[512,1024]{1,0:T(8,128)(2,1)}, u32[]{:S(2)}, u32[]{:S(2)}) %collective-permute-start.32) | collective-permute-done | bytes 1048608 | tf_op jit(solution)/shard_map/ppermute | solution.py:51
  1567.7 18.5 %collective-permute-done.26 = bf16[512,1024]{1,0:T(8,128)(2,1)S(1)} collective-permute-done((bf16[512,1024]{1,0:T(8,128)(2,1)S(1)}, bf16[512,1024]{1,0:T(8,128)(2,1)S(1)}, u32[]{:S(2)}, u32[]{:S(2)}) %collective-permute-start.26) | collective-permute-done | bytes 1048608 | tf_op jit(solution)/shard_map/ppermute | solution.py:51
  1589.0 19.9 %collective-permute-done.27 = bf16[512,1024]{1,0:T(8,128)(2,1)S(1)} collective-permute-done((bf16[512,1024]{1,0:T(8,128)(2,1)S(1)}, bf16[512,1024]{1,0:T(8,128)(2,1)S(1)}, u32[]{:S(2)}, u32[]{:S(2)}) %collective-permute-start.27) | collective-permute-done | bytes 1048608 | tf_op jit(solution)/shard_map/ppermute | solution.py:51
  1657.3 13.5 psum.39
  (305 shorter events, 326.0 us)
Async XLA Ops:
  7.2 169.5 %all-gather.5.cloned.1.call-start = ((), (), s32[]{:S(2)}) async-start(), calls=%async_computation.4 | async-start | bytes 10485760 | tf_op jit(solution)/shard_map/all_gather | solution.py:40
  28.7 297.9 %all-gather.7.cloned.1.call-start = ((), (), s32[]{:S(2)}) async-start(), calls=%async_computation.5 | async-start | bytes 10485760 | tf_op jit(solution)/shard_map/all_gather | solution.py:40
  176.7 295.0 %reduce-scatter.5.cloned.1.call-start = ((), (), s32[]{:S(2)}) async-start(), calls=%async_computation.6 | async-start | bytes 10485760 | tf_op jit(solution)/shard_map/reduce_scatter | solution.py:44
  176.9 64.0 %collective-permute-start = (bf16[512,768]{1,0:T(8,128)(2,1)S(1)}, bf16[512,768]{1,0:T(8,128)(2,1)}, u32[]{:S(2)}, u32[]{:S(2)}) collective-permute-start(bf16[512,768]{1,0:T(8,128)(2,1)S(1)} %constant_dynamic-update-slice_fusion.30), channel_id=1, source_target_pairs={{0,1},{1,0},{2,3},{3,2},{4,5},{5,4},{6,7},{7,6},{8,9},{9,8},{10,11... | collective-permute-start | bytes 2359304 | tf_op jit(solution)/shard_map/ppermute | solution.py:51
  178.4 63.7 %collective-permute-start.1 = (bf16[512,768]{1,0:T(8,128)(2,1)S(1)}, bf16[512,768]{1,0:T(8,128)(2,1)}, u32[]{:S(2)}, u32[]{:S(2)}) collective-permute-start(bf16[512,768]{1,0:T(8,128)(2,1)S(1)} %constant_dynamic-update-slice_fusion.30), channel_id=1, source_target_pairs={{0,2},{1,3},{2,0},{3,1},{4,6},{5,7},{6,4},{7,5},{8,10},{9,11},{10,... | collective-permute-start | bytes 2359304 | tf_op jit(solution)/shard_map/ppermute | solution.py:51
  180.5 56.6 %collective-permute-start.4 = (bf16[512,512]{1,0:T(8,128)(2,1)S(1)}, bf16[512,512]{1,0:T(8,128)(2,1)}, u32[]{:S(2)}, u32[]{:S(2)}) collective-permute-start(bf16[512,512]{1,0:T(8,128)(2,1)S(1)} %copy-done.35), channel_id=1, source_target_pairs={{0,2},{1,3},{2,0},{3,1},{4,6},{5,7},{6,4},{7,5},{8,10},{9,11},{10,... | collective-permute-start | bytes 1572872 | tf_op jit(solution)/shard_map/ppermute | solution.py:51
  181.0 58.0 %collective-permute-start.5 = (bf16[512,512]{1,0:T(8,128)(2,1)S(1)}, bf16[512,512]{1,0:T(8,128)(2,1)}, u32[]{:S(2)}, u32[]{:S(2)}) collective-permute-start(bf16[512,512]{1,0:T(8,128)(2,1)S(1)} %copy-done.35), channel_id=1, source_target_pairs={{0,3},{1,2},{2,1},{3,0},{4,7},{5,6},{6,5},{7,4},{8,11},{9,10},{10,... | collective-permute-start | bytes 1572872 | tf_op jit(solution)/shard_map/ppermute | solution.py:51
  326.7 464.5 %all-gather.9.cloned.1.call-start = ((), (), s32[]{:S(2)}) async-start(), calls=%async_computation.7 | async-start | bytes 10485760 | tf_op jit(solution)/shard_map/all_gather | solution.py:40
  493.6 549.9 %reduce-scatter.9.cloned.1.call-start = ((), (), s32[]{:S(2)}) async-start(), calls=%async_computation.9 | async-start | bytes 10485760 | tf_op jit(solution)/shard_map/reduce_scatter | solution.py:44
  493.9 48.8 %collective-permute-start.9 = (bf16[512,2048]{1,0:T(8,128)(2,1)}, bf16[512,2048]{1,0:T(8,128)(2,1)S(1)}, u32[]{:S(2)}, u32[]{:S(2)}) collective-permute-start(bf16[512,2048]{1,0:T(8,128)(2,1)} %param.20), channel_id=1, source_target_pairs={{0,1},{1,0},{2,3},{3,2},{4,5},{5,4},{6,7},{7,6},{8,9},{9,8},{10,11... | collective-permute-start | bytes 6291464 | tf_op jit(solution)/shard_map/ppermute | solution.py:51
  495.6 93.7 %collective-permute-start.10 = (bf16[512,2048]{1,0:T(8,128)(2,1)}, bf16[512,2048]{1,0:T(8,128)(2,1)S(1)}, u32[]{:S(2)}, u32[]{:S(2)}) collective-permute-start(bf16[512,2048]{1,0:T(8,128)(2,1)} %param.20), channel_id=1, source_target_pairs={{0,2},{1,3},{2,0},{3,1},{4,6},{5,7},{6,4},{7,5},{8,10},{9,11},{10,... | collective-permute-start | bytes 6291464 | tf_op jit(solution)/shard_map/ppermute | solution.py:51
  497.1 95.0 %collective-permute-start.11 = (bf16[512,2048]{1,0:T(8,128)(2,1)}, bf16[512,2048]{1,0:T(8,128)(2,1)}, u32[]{:S(2)}, u32[]{:S(2)}) collective-permute-start(bf16[512,2048]{1,0:T(8,128)(2,1)} %param.20), channel_id=1, source_target_pairs={{0,3},{1,2},{2,1},{3,0},{4,7},{5,6},{6,5},{7,4},{8,11},{9,10},{10,... | collective-permute-start | bytes 6291464 | tf_op jit(solution)/shard_map/ppermute | solution.py:51
  497.4 135.3 %collective-permute-start.12 = (bf16[2048,512]{1,0:T(8,128)(2,1)}, bf16[2048,512]{1,0:T(8,128)(2,1)}, u32[]{:S(2)}, u32[]{:S(2)}) collective-permute-start(bf16[2048,512]{1,0:T(8,128)(2,1)} %param.21), channel_id=1, source_target_pairs={{0,1},{1,0},{2,3},{3,2},{4,5},{5,4},{6,7},{7,6},{8,9},{9,8},{10,11... | collective-permute-start | bytes 6291464 | tf_op jit(solution)/shard_map/ppermute | solution.py:51
  499.1 180.2 %collective-permute-start.13 = (bf16[2048,512]{1,0:T(8,128)(2,1)}, bf16[2048,512]{1,0:T(8,128)(2,1)}, u32[]{:S(2)}, u32[]{:S(2)}) collective-permute-start(bf16[2048,512]{1,0:T(8,128)(2,1)} %param.21), channel_id=1, source_target_pairs={{0,2},{1,3},{2,0},{3,1},{4,6},{5,7},{6,4},{7,5},{8,10},{9,11},{10,... | collective-permute-start | bytes 6291464 | tf_op jit(solution)/shard_map/ppermute | solution.py:51
  544.0 137.3 %collective-permute-start.14 = (bf16[2048,512]{1,0:T(8,128)(2,1)}, bf16[2048,512]{1,0:T(8,128)(2,1)}, u32[]{:S(2)}, u32[]{:S(2)}) collective-permute-start(bf16[2048,512]{1,0:T(8,128)(2,1)} %param.21), channel_id=1, source_target_pairs={{0,3},{1,2},{2,1},{3,0},{4,7},{5,6},{6,5},{7,4},{8,11},{9,10},{10,... | collective-permute-start | bytes 6291464 | tf_op jit(solution)/shard_map/ppermute | solution.py:51
  590.7 132.0 %collective-permute-start.6 = (bf16[512,2048]{1,0:T(8,128)(2,1)}, bf16[512,2048]{1,0:T(8,128)(2,1)}, u32[]{:S(2)}, u32[]{:S(2)}) collective-permute-start(bf16[512,2048]{1,0:T(8,128)(2,1)} %param.19), channel_id=1, source_target_pairs={{0,1},{1,0},{2,3},{3,2},{4,5},{5,4},{6,7},{7,6},{8,9},{9,8},{10,11... | collective-permute-start | bytes 6291464 | tf_op jit(solution)/shard_map/ppermute | solution.py:51
  592.1 173.7 %collective-permute-start.7 = (bf16[512,2048]{1,0:T(8,128)(2,1)}, bf16[512,2048]{1,0:T(8,128)(2,1)}, u32[]{:S(2)}, u32[]{:S(2)}) collective-permute-start(bf16[512,2048]{1,0:T(8,128)(2,1)} %param.19), channel_id=1, source_target_pairs={{0,2},{1,3},{2,0},{3,1},{4,6},{5,7},{6,4},{7,5},{8,10},{9,11},{10,... | collective-permute-start | bytes 6291464 | tf_op jit(solution)/shard_map/ppermute | solution.py:51
  632.7 136.2 %collective-permute-start.8 = (bf16[512,2048]{1,0:T(8,128)(2,1)}, bf16[512,2048]{1,0:T(8,128)(2,1)S(1)}, u32[]{:S(2)}, u32[]{:S(2)}) collective-permute-start(bf16[512,2048]{1,0:T(8,128)(2,1)} %param.19), channel_id=1, source_target_pairs={{0,3},{1,2},{2,1},{3,0},{4,7},{5,6},{6,5},{7,4},{8,11},{9,10},{10,... | collective-permute-start | bytes 6291464 | tf_op jit(solution)/shard_map/ppermute | solution.py:51
  901.6 289.5 %reduce-scatter.7.cloned.1.call-start = ((), (), s32[]{:S(2)}) async-start(), calls=%async_computation.8 | async-start | bytes 10485760 | tf_op jit(solution)/shard_map/reduce_scatter | solution.py:44
  926.0 423.5 %all-gather.11.cloned.1.call-start = ((), (), s32[]{:S(2)}) async-start(), calls=%async_computation.10 | async-start | bytes 10485760 | tf_op jit(solution)/shard_map/all_gather | solution.py:40
  1199.0 454.3 %reduce-scatter.11.cloned.1.call-start = ((), (), s32[]{:S(2)}) async-start(), calls=%async_computation.11 | async-start | bytes 10485760 | tf_op jit(solution)/shard_map/reduce_scatter | solution.py:44
  1228.0 234.6 %collective-permute-start.35 = (bf16[1024,2048]{1,0:T(8,128)(2,1)}, bf16[1024,2048]{1,0:T(8,128)(2,1)}, u32[]{:S(2)}, u32[]{:S(2)}) collective-permute-start(bf16[1024,2048]{1,0:T(8,128)(2,1)} %constant_dynamic-slice_fusion.3), channel_id=1, source_target_pairs={{0,16},{16,0},{1,17},{17,1},{2,18},{18,2},{3,19},{19,3},{4,20},{20... | collective-permute-start | bytes 12582920 | tf_op jit(solution)/shard_map/ppermute | solution.py:51
  1471.5 48.7 %collective-permute-start.37 = (bf16[1024,512]{1,0:T(8,128)(2,1)}, bf16[1024,512]{1,0:T(8,128)(2,1)S(1)}, u32[]{:S(2)}, u32[]{:S(2)}) collective-permute-start(bf16[1024,512]{1,0:T(8,128)(2,1)} %get-tuple-element.58), channel_id=1, source_target_pairs={{0,2},{1,3},{2,0},{3,1},{4,6},{5,7},{6,4},{7,5},{8,10},{9,11},{10,... | collective-permute-start | bytes 3145736 | tf_op jit(solution)/shard_map/ppermute | solution.py:51
  1473.0 55.8 %collective-permute-start.38 = (bf16[1024,512]{1,0:T(8,128)(2,1)}, bf16[1024,512]{1,0:T(8,128)(2,1)S(1)}, u32[]{:S(2)}, u32[]{:S(2)}) collective-permute-start(bf16[1024,512]{1,0:T(8,128)(2,1)} %get-tuple-element.57), channel_id=1, source_target_pairs={{0,3},{1,2},{2,1},{3,0},{4,7},{5,6},{6,5},{7,4},{8,11},{9,10},{10,... | collective-permute-start | bytes 3145736 | tf_op jit(solution)/shard_map/ppermute | solution.py:51
  1480.9 60.3 %collective-permute-start.31 = (bf16[512,1024]{1,0:T(8,128)(2,1)}, bf16[512,1024]{1,0:T(8,128)(2,1)S(1)}, u32[]{:S(2)}, u32[]{:S(2)}) collective-permute-start(bf16[512,1024]{1,0:T(8,128)(2,1)} %get-tuple-element.59), channel_id=1, source_target_pairs={{0,1},{1,0},{2,3},{3,2},{4,5},{5,4},{6,7},{7,6},{8,9},{9,8},{10,11... | collective-permute-start | bytes 3145736 | tf_op jit(solution)/shard_map/ppermute | solution.py:51
  1482.4 82.9 %collective-permute-start.32 = (bf16[512,1024]{1,0:T(8,128)(2,1)}, bf16[512,1024]{1,0:T(8,128)(2,1)}, u32[]{:S(2)}, u32[]{:S(2)}) collective-permute-start(bf16[512,1024]{1,0:T(8,128)(2,1)} %get-tuple-element.61), channel_id=1, source_target_pairs={{0,2},{1,3},{2,0},{3,1},{4,6},{5,7},{6,4},{7,5},{8,10},{9,11},{10,... | collective-permute-start | bytes 3145736 | tf_op jit(solution)/shard_map/ppermute | solution.py:51
  1500.1 65.2 %collective-permute-start.33 = (bf16[512,1024]{1,0:T(8,128)(2,1)S(1)}, bf16[512,1024]{1,0:T(8,128)(2,1)S(1)}, u32[]{:S(2)}, u32[]{:S(2)}) collective-permute-start(bf16[512,1024]{1,0:T(8,128)(2,1)S(1)} %copy-done.29), channel_id=1, source_target_pairs={{0,3},{1,2},{2,1},{3,0},{4,7},{5,6},{6,5},{7,4},{8,11},{9,10},{10,... | collective-permute-start | bytes 3145736 | tf_op jit(solution)/shard_map/ppermute | solution.py:51
  1520.2 66.0 %collective-permute-start.26 = (bf16[512,1024]{1,0:T(8,128)(2,1)S(1)}, bf16[512,1024]{1,0:T(8,128)(2,1)S(1)}, u32[]{:S(2)}, u32[]{:S(2)}) collective-permute-start(bf16[512,1024]{1,0:T(8,128)(2,1)S(1)} %get-tuple-element.62), channel_id=1, source_target_pairs={{0,1},{1,0},{2,3},{3,2},{4,5},{5,4},{6,7},{7,6},{8,9},{9,8},{10,11... | collective-permute-start | bytes 3145736 | tf_op jit(solution)/shard_map/ppermute | solution.py:51
  1528.8 80.1 %collective-permute-start.27 = (bf16[512,1024]{1,0:T(8,128)(2,1)S(1)}, bf16[512,1024]{1,0:T(8,128)(2,1)S(1)}, u32[]{:S(2)}, u32[]{:S(2)}) collective-permute-start(bf16[512,1024]{1,0:T(8,128)(2,1)S(1)} %get-tuple-element.64), channel_id=1, source_target_pairs={{0,2},{1,3},{2,0},{3,1},{4,6},{5,7},{6,4},{7,5},{8,10},{9,11},{10,... | collective-permute-start | bytes 3145736 | tf_op jit(solution)/shard_map/ppermute | solution.py:51
  1541.2 67.7 %collective-permute-start.28 = (bf16[512,1024]{1,0:T(8,128)(2,1)S(1)}, bf16[512,1024]{1,0:T(8,128)(2,1)}, u32[]{:S(2)}, u32[]{:S(2)}) collective-permute-start(bf16[512,1024]{1,0:T(8,128)(2,1)S(1)} %get-tuple-element.63), channel_id=1, source_target_pairs={{0,3},{1,2},{2,1},{3,0},{4,7},{5,6},{6,5},{7,4},{8,11},{9,10},{10,... | collective-permute-start | bytes 3145736 | tf_op jit(solution)/shard_map/ppermute | solution.py:51
  1565.3 46.6 %collective-permute-start.20 = (bf16[256,2048]{1,0:T(8,128)(2,1)S(1)}, bf16[256,2048]{1,0:T(8,128)(2,1)S(1)}, u32[]{:S(2)}, u32[]{:S(2)}) collective-permute-start(bf16[256,2048]{1,0:T(8,128)(2,1)S(1)} %constant_dynamic-slice_fusion.15), channel_id=1, source_target_pairs={{0,16},{16,0},{1,17},{17,1},{2,18},{18,2},{3,19},{19,3},{4,20},{20... | collective-permute-start | bytes 3145736 | tf_op jit(solution)/shard_map/ppermute | solution.py:51
  1565.3 49.2 %collective-permute-start.15 = (bf16[2048,384]{1,0:T(8,128)(2,1)S(1)}, bf16[2048,384]{1,0:T(8,128)(2,1)S(1)}, u32[]{:S(2)}, u32[]{:S(2)}) collective-permute-start(bf16[2048,384]{1,0:T(8,128)(2,1)S(1)} %constant_dynamic-slice_fusion.19), channel_id=1, source_target_pairs={{0,16},{16,0},{1,17},{17,1},{2,18},{18,2},{3,19},{19,3},{4,20},{20... | collective-permute-start | bytes 4718600 | tf_op jit(solution)/shard_map/ppermute | solution.py:51
  (72 other events, 3009.7 us)
Sparse Core Ops, SparseCore 0:
  28.8 147.8 all-gather.4
  178.8 147.8 all-gather.6
  329.0 142.6 reduce-scatter.4
  493.7 148.0 all-gather.8
  901.7 141.7 reduce-scatter.8
  1045.7 145.3 reduce-scatter.6
  1199.1 150.3 all-gather.10
  1430.2 142.6 reduce-scatter.10
